TPU v7x, 128 devices: a whole 4x4x4 slice. The times are simulated.
128 devices in a mesh: row: 8 (over x, y_hi), col: 16 (over y_lo, z, core).
Axes of the slice: x: 4, y: 4 (y_hi: 2, y_lo: 2; y = y_hi * 2 + y_lo), z: 4, core: 2. Of those that a mesh axis runs over, the one named last changes fastest.
Arguments:
- selected_inverse: bfloat16 [20480, 20480], P('row', 'col'), may hold values from -6 to 6
- pattern: int32 [160, 160], P('row', 'col'), may hold values 0 or 1
- ltil: bfloat16 [20480, 2048], P('row', 'col'), may hold values from -0.0390625 to 0.0390625
- diag_inverse: float32 [2048, 2048], P('row', 'col'), may hold values from -6 to 6
Outputs:
- panel: bfloat16 [20480, 2048], P('row', 'col')
- corner: float32 [2048, 2048], P('row', 'col')
All inputs are finite; a program needn't handle non-finite values. No bound on the sum of `pattern` on one device may be relied on, other than what follows from the above.
Results may differ from a plain program's by a relative error of at most 0.0021.
Values may be sent and summed in bfloat16 or wider, within the bound.
A program may use at most 128 MiB of HBM per device.

v0:
```python
import jax
import jax.numpy as jnp
from jax import lax
from jax.sharding import PartitionSpec as P

BLK = 128


def local(selected_inverse, pattern, ltil, diag_inverse):
    local_rows, local_cols = selected_inverse.shape
    masked = (
        selected_inverse.reshape(pattern.shape[0], BLK, pattern.shape[1], BLK)
        * pattern[:, None, :, None].astype(jnp.bfloat16)
    ).reshape(local_rows, local_cols)
    tall = lax.all_gather(ltil, "row", axis=0, tiled=True)
    matched = lax.all_to_all(tall, "col", split_axis=0, concat_axis=1, tiled=True)
    partial_panel = jnp.dot(masked, matched, preferred_element_type=jnp.float32)
    summed = lax.psum_scatter(partial_panel, "col", scatter_dimension=1, tiled=True)
    panel = (-summed).astype(jnp.bfloat16)
    corner_part = lax.dot_general(
        lax.all_gather(ltil, "col", axis=1, tiled=True),
        panel,
        (((0,), (0,)), ((), ())),
        preferred_element_type=jnp.float32,
    )
    corner = diag_inverse - lax.psum_scatter(corner_part, "row", scatter_dimension=0, tiled=True)
    return (panel, corner)


def solution(mesh):
    placed = (P("row", "col"), P("row", "col"), P("row", "col"), P("row", "col"))
    return jax.shard_map(
        local,
        mesh=mesh,
        in_specs=placed,
        out_specs=(P("row", "col"), P("row", "col")),
        check_vma=False,
    )
```

profile of v0, /device:TPU:102, one launch (start us, length us, event | category | flops | bytes accessed | tf_op | source)
XLA Modules:
  0.0 485.5 jit_solution(11954163736313903091)
XLA Ops:
  7.2 0.0 copy-start.2
  7.2 0.0 all-gather.3.cloned.1.call-start
  7.2 0.7 all-gather.3.cloned.1.call-update
  7.9 82.1 %all-gather.3.cloned.1.call-done = bf16[20480,128]{1,0:T(8,128)(2,1)} async-done(((bf16[2560,128]{1,0:T(8,128)(2,1)}), bf16[20480,128]{1,0:T(8,128)(2,1)}) %all-gather.3.cloned.1.call-update) | async-done | bytes 5242896 | tf_op jit(solution)/shard_map/all_gather | solution.py:15
  90.0 4.8 all-to-all-start
  94.7 0.0 reduce-scatter.3.cloned.1.call-start
  94.8 0.0 copy-done.2
  94.8 9.5 %copy.12 = bf16[2560,1280]{0,1:T(8,128)(2,1)} copy(bf16[2560,1280]{1,0:T(8,128)(2,1)} %param.4) | data formatting | bytes 13107200 | tf_op args[0]
  104.3 68.5 %all-to-all-done = bf16[16,1280,128]{2,1,0:T(8,128)(2,1)} async-done(((bf16[16,1280,128]{2,1,0:T(8,128)(2,1)}), bf16[16,1280,128]{2,1,0:T(8,128)(2,1)}, u32[]{:S(2)}, u32[]{:S(2)}) %all-to-all-start) | async-done | bytes 5242912 | tf_op jit(solution)/shard_map/all_to_all | solution.py:16
  172.8 7.9 %copy.13 = bf16[1280,16,128]{0,2,1:T(8,128)(2,1)} copy(bf16[1280,16,128]{2,0,1:T(8,128)(2,1)} %bitcast.1) | data formatting | bytes 10485760 | tf_op jit(solution)/shard_map/all_to_all | solution.py:16
  180.7 4.2 mul.11
  184.9 24.0 %fusion = f32[2560,2048]{1,0:T(8,128)} fusion(bf16[1280,2048]{0,1:T(8,128)(2,1)} %bitcast.17, bf16[2560,1280]{0,1:T(8,128)(2,1)} %copy.12, bf16[160,8,20,128]{3,2,1,0:T(8,128)(2,1)} %bitcast.15), kind=kOutput, calls=%fused_computation.1 | convolution fusion | flops 13425049600 | bytes 39321600 | tf_op jit(solution)/shard_map/dot_general | solution.py:17
  208.8 0.0 reduce-scatter.3.cloned.1.call-update
  208.9 0.0 all-gather.5.cloned.1.call-start
  208.9 0.7 all-gather.5.cloned.1.call-update
  209.6 0.0 reduce-scatter.5.cloned.1.call-start
  209.6 116.5 %reduce-scatter.3.cloned.1.call-done = f32[2560,128]{1,0:T(8,128)} async-done(((f32[2560,2048]{1,0:T(8,128)}), f32[2560,128]{1,0:T(8,128)}) %reduce-scatter.3.cloned.1.call-update) | async-done | bytes 1310736 | tf_op jit(solution)/shard_map/reduce_scatter | solution.py:18
  326.1 1.4 negate_convert_fusion
  327.5 0.0 copy-start
  327.5 0.0 copy-start.1
  327.5 70.1 %all-gather.5.cloned.1.call-done = bf16[2560,2048]{1,0:T(8,128)(2,1)} async-done(((bf16[2560,128]{1,0:T(8,128)(2,1)}), bf16[2560,2048]{1,0:T(8,128)(2,1)}) %all-gather.5.cloned.1.call-update) | async-done | bytes 10485776 | tf_op jit(solution)/shard_map/all_gather | solution.py:21
  397.7 6.5 %convolution_bitcast_fusion = f32[2048,128]{0,1:T(8,128)} fusion(bf16[2560,128]{1,0:T(8,128)(2,1)S(1)} %negate_convert_fusion, bf16[2560,2048]{1,0:T(8,128)(2,1)} %all-gather.5.cloned.1.call-done), kind=kOutput, calls=%fused_computation.3 | convolution fusion | flops 1342177280 | bytes 12189696 | tf_op jit(solution)/shard_map/dot_general | solution.py:20
  404.2 0.0 copy-done
  404.2 0.0 reduce-scatter.5.cloned.1.call-update
  404.2 0.0 copy-done.1
  404.2 0.1 copy.14
  404.3 73.0 %reduce-scatter.5.cloned.1.call-done = f32[256,128]{0,1:T(8,128)} async-done(((f32[2048,128]{0,1:T(8,128)}), f32[256,128]{0,1:T(8,128)}) %reduce-scatter.5.cloned.1.call-update) | async-done | bytes 131088 | tf_op jit(solution)/shard_map/reduce_scatter | solution.py:26
  477.3 0.9 sub.3
  478.3 0.8 copy.15
  (1 shorter events, 0.0 us)
Async XLA Ops:
  7.2 87.6 %copy-start.2 = (s32[20,10]{0,1:T(8,128)S(1)}, s32[20,10]{0,1:T(8,128)}, u32[]{:S(2)}) copy-start(s32[20,10]{0,1:T(8,128)} %param.5) | copy-start | bytes 2404
  7.2 82.8 %all-gather.3.cloned.1.call-start = ((), (), s32[]{:S(2)}) async-start(), calls=%async_computation.3 | async-start | bytes 5898240 | tf_op jit(solution)/shard_map/all_gather | solution.py:15
  90.0 82.8 %all-to-all-start = ((bf16[16,1280,128]{2,1,0:T(8,128)(2,1)}), bf16[16,1280,128]{2,1,0:T(8,128)(2,1)}, u32[]{:S(2)}, u32[]{:S(2)}) async-start(bf16[16,1280,128]{2,1,0:T(8,128)(2,1)} %bitcast.16), calls=%async_computation | async-start | bytes 10485760 | tf_op jit(solution)/shard_map/all_to_all | solution.py:16
  94.7 231.4 %reduce-scatter.3.cloned.1.call-start = ((), (), s32[]{:S(2)}) async-start(), calls=%async_computation.4 | async-start | bytes 22282240 | tf_op jit(solution)/shard_map/reduce_scatter | solution.py:18
  208.9 188.8 %all-gather.5.cloned.1.call-start = ((), (), s32[]{:S(2)}) async-start(), calls=%async_computation.5 | async-start | bytes 11141120 | tf_op jit(solution)/shard_map/all_gather | solution.py:21
  209.6 267.7 %reduce-scatter.5.cloned.1.call-start = ((), (), s32[]{:S(2)}) async-start(), calls=%async_computation.6 | async-start | bytes 1179648 | tf_op jit(solution)/shard_map/reduce_scatter | solution.py:26
  327.5 76.7 %copy-start = (bf16[2560,128]{1,0:T(8,128)(2,1)}, bf16[2560,128]{1,0:T(8,128)(2,1)S(1)}, u32[]{:S(2)}) copy-start(bf16[2560,128]{1,0:T(8,128)(2,1)S(1)} %negate_convert_fusion) | copy-start | bytes 1966084
  327.5 76.7 %copy-start.1 = (f32[256,128]{1,0:T(8,128)S(1)}, f32[256,128]{1,0:T(8,128)}, u32[]{:S(2)}) copy-start(f32[256,128]{1,0:T(8,128)} %param.7) | copy-start | bytes 393220
Sparse Core Ops, SparseCore 0:
  10.3 79.5 all-gather.2
  209.0 117.0 reduce-scatter.2
  327.7 69.8 all-gather.4
  404.3 72.9 reduce-scatter.4
where the time goes:
time: 488 us; the launch traced here: 486 us
  waiting for transfers between devices  412 us (84%)
  matrix products  30.5 us (6%)
  local copies, waits for them, and re-layouts  22.5 us (5%)
  between operations  13.8 us (3%)
  starting transfers between devices  4.91 us (1%)
    reduce_scatter x1, waiting for transfers between devices, local(): lax.psum_scatter(partial_panel, 'col', scatter_dimension=1, tiled=True)  116 us
    all_gather x1, waiting for transfers between devices, local(): tall = lax.all_gather(ltil, 'row', axis=0, tiled=True)  82.1 us
    reduce_scatter x1, waiting for transfers between devices, local(): lax.psum_scatter(corner_part, 'row', scatter_dimension=0, tiled=True)  73 us
    all_gather x1, waiting for transfers between devices, local(): lax.all_gather(ltil, 'col', axis=1, tiled=True)  70.1 us
    all_to_all x1, waiting for transfers between devices, local(): lax.all_to_all(tall, 'col', split_axis=0, concat_axis=1, tiled=True)  68.5 us
    dot_general x1, matrix products, local(): partial_panel = jnp.dot(masked, matched, preferred_element_type=jnp.float32)  24 us
    unnamed x9, local copies, waits for them, and re-layouts  10.4 us
  transfers between devices with their start and end apart: 5, of which 5 were waited for; matrix products, arithmetic and copies ran while one was open for 2% of the time, Pallas kernels for 0%

commit v1 on v0

v1 whole, which is shorter than its diff:
```python
import functools

import jax
import jax.numpy as jnp
from jax import lax
from jax.experimental import pallas as pl
from jax.experimental.pallas import tpu as pltpu
from jax.sharding import PartitionSpec as P

MESH = pl.DeviceIdType.MESH
BLK = 128
ROWS = 2560
HALF = 1280
TILE = 512
PACKED = 16
F32 = jnp.float32


def device(r, c, k):
    return (r, c * 2 + k)


def kernel(
    a_ref, pat_ref, lt_ref, diag_ref,
    panel_ref, corner_ref,
    a_all, b_all, total, q_out, q_in, mine, slabs, part, parts_in,
    a_sem, core_send, core_recv, first_send, first_recv, pair_send, pair_recv,
    x_send, x_recv, sum_send, sum_recv, slab_send, slab_recv, part_send, part_recv,
):
    r = lax.axis_index("row")
    col = lax.axis_index("col")
    c, k = col // 2, col % 2
    x, yh = r // 2, r % 2
    yl, z = c // 4, c % 4

    def xor(a, b, bits):
        out = 0
        for i in range(bits):
            w = 1 << i
            out = out + w * (((a // w) + (b // w)) % 2)
        return out

    rc = xor(r, c, 3)
    ahead = {1: (x + 1) % 4, 2: (x + 3) % 4, 3: (x + 2) % 4}
    behind = {1: (x + 3) % 4, 2: (x + 1) % 4, 3: (x + 2) % 4}

    barrier = pltpu.get_barrier_semaphore()
    senders = [device(c, rc, k), device(r, c, 1 - k), device(x * 2 + 1 - yh, c, k)]
    senders += [device(behind[d] * 2 + yh, c, k) for d in (1, 2, 3)]
    for i in range(1, 8):
        senders.append(device(r, ((yl + i // 4) % 2) * 4 + (z + 4 - i % 4) % 4, k))
    for b in range(8):
        for kk in range(2):
            senders.append(device(xor(c, b, 3), b, kk))
    for s in senders:
        pl.semaphore_signal(barrier, inc=1, device_id=s, device_id_type=MESH)

    own_a = pltpu.make_async_copy(a_ref, a_all.at[k], a_sem.at[0])
    own_a.start()
    pl.semaphore_wait(barrier, len(senders))

    def remote(src, dst, send, recv, to):
        return pltpu.make_async_remote_copy(
            src_ref=src, dst_ref=dst, send_sem=send, recv_sem=recv, device_id=to, device_id_type=MESH
        )

    stays = jnp.logical_and(r == 0, c == 0)
    first = remote(lt_ref, b_all.at[0], first_send.at[0], first_recv.at[0], device(rc, r, k))

    @pl.when(jnp.logical_not(stays))
    def _():
        first.start()

    @pl.when(stays)
    def _():
        pltpu.make_async_copy(lt_ref, b_all.at[0], first_recv.at[0]).start()

    own_a.wait()

    def mask(i, carry):
        rows = pl.ds(pl.multiple_of(i * BLK, BLK), BLK)
        for j in range(HALF // BLK):
            keep = jnp.full((BLK, BLK), pat_ref[i, j].astype(F32), F32).astype(jnp.bfloat16)
            cols = slice(j * BLK, (j + 1) * BLK)
            a_all[k, rows, cols] = a_all[k, rows, cols] * keep
        return carry

    lax.fori_loop(0, ROWS // BLK, mask, 0)
    swap = remote(a_all.at[k], a_all.at[k], core_send.at[0], core_recv.at[0], device(r, c, 1 - k))
    swap.start()

    first.wait_recv()
    pair = remote(b_all.at[0], b_all.at[1], pair_send.at[0], pair_recv.at[0], device(x * 2 + 1 - yh, c, k))
    pair.start()
    gather = {}
    for d in (1, 2, 3):
        for h in range(2):
            gather[d, h] = remote(
                b_all.at[h], b_all.at[2 * d + h], x_send.at[2 * (d - 1) + h], x_recv.at[2 * (d - 1) + h],
                device(ahead[d] * 2 + yh, c, k),
            )
    gather[1, 0].start()
    gather[2, 0].start()
    pair.wait_recv()
    gather[1, 1].start()
    gather[2, 1].start()
    gather[3, 0].start()
    gather[3, 1].start()

    remote(a_all.at[1 - k], a_all.at[1 - k], core_send.at[0], core_recv.at[0], device(r, c, 1 - k)).wait_recv()

    def slab_of(d, h):
        row = (x if d == 0 else behind[d]) * 2 + (yh if h == 0 else 1 - yh)
        return xor(row, c, 3)

    def send_of(i, dst_col):
        return remote(q_out.at[i], q_in.at[i], sum_send.at[i], sum_recv.at[i], device(r, dst_col, k))

    for d in range(4):
        if d:
            gather[d, 0].wait_recv()
            gather[d, 1].wait_recv()
        right = [
            jnp.concatenate([b_all[2 * d, s, :], b_all[2 * d + 1, s, :]], axis=1)
            for s in (slice(0, HALF), slice(HALF, ROWS))
        ]

        def multiply(t, most, right=right):
            rows = pl.ds(pl.multiple_of(t * TILE, TILE), TILE)
            out = jnp.dot(a_all[0, rows, :], right[0], preferred_element_type=F32)
            out = out + jnp.dot(a_all[1, rows, :], right[1], preferred_element_type=F32)
            total[rows, :] = out
            return jnp.maximum(most, jnp.max(jnp.abs(out), axis=0, keepdims=True))

        most = lax.fori_loop(0, ROWS // TILE, multiply, jnp.zeros((1, 2 * BLK), F32))
        power = jnp.clip(jnp.floor(jnp.log2(32000.0 / most)), -120.0, 120.0)
        scale = jnp.exp2(power)
        slot = []
        for h in range(2):
            s = slab_of(d, h)
            slot.append(((yl + s // 4) % 2) * 4 + (s % 4 + 4 - z) % 4)

        def narrow(t, carry, scale=scale, slot=slot):
            rows = pl.ds(pl.multiple_of(t * TILE, TILE), TILE)
            scaled = (total[rows, :] * scale).astype(jnp.int32).astype(jnp.int16)
            for h in range(2):
                q_out[slot[h], rows, :] = scaled[:, h * BLK:(h + 1) * BLK]
            return carry

        lax.fori_loop(0, ROWS // TILE, narrow, 0)
        code = jnp.broadcast_to(power, (PACKED, 2 * BLK)).astype(jnp.int32).astype(jnp.int16)
        for h in range(2):
            q_out[slot[h], ROWS:, :] = code[:, h * BLK:(h + 1) * BLK]
            @pl.when(slot[h] != 0)
            def _(h=h, d=d):
                send_of(slot[h], slab_of(d, h)).start()

    for i in range(1, 8):
        send_of(i, c).wait_recv()

    def unit(ref, i):
        return jnp.exp2(-ref[i, ROWS:, :].astype(jnp.int32).astype(F32)[0:1, :])

    units = [unit(q_out, 0)] + [unit(q_in, i) for i in range(1, 8)]

    def add(t, carry):
        rows = pl.ds(pl.multiple_of(t * BLK, BLK), BLK)
        out = q_out[0, rows, :].astype(jnp.int32).astype(F32) * units[0]
        for i in range(1, 8):
            out = out + q_in[i, rows, :].astype(jnp.int32).astype(F32) * units[i]
        mine[rows, :] = (-out).astype(jnp.bfloat16)
        panel_ref[rows, :] = (-out).astype(jnp.bfloat16)
        return carry

    lax.fori_loop(0, ROWS // BLK, add, 0)

    third = remote(mine, slabs.at[k], slab_send.at[0], slab_recv.at[0], device(rc, r, k))

    @pl.when(jnp.logical_not(stays))
    def _():
        third.start()

    @pl.when(stays)
    def _():
        pltpu.make_async_copy(mine, slabs.at[k], slab_recv.at[0]).start()

    third.wait_recv()
    share = remote(slabs.at[k], slabs.at[k], slab_send.at[1], slab_recv.at[1], device(r, c, 1 - k))
    share.start()
    remote(slabs.at[1 - k], slabs.at[1 - k], slab_send.at[1], slab_recv.at[1], device(r, c, 1 - k)).wait_recv()

    def corner_of(j, kk):
        to = slab_of(j // 2, j % 2)
        own = jnp.logical_and(jnp.logical_and(to == r, rc == c), k == kk)
        copy = remote(
            part.at[j, kk], parts_in.at[c, k], part_send.at[j, kk], part_recv.at[c, k], device(to, rc, kk)
        )
        return own, copy

    for j in range(8):
        for kk in range(2):
            part[j, kk] = lax.dot_general(
                b_all[j], slabs[kk], (((0,), (0,)), ((), ())), preferred_element_type=F32
            )
            own, copy = corner_of(j, kk)

            @pl.when(own)
            def _(j=j, kk=kk):
                parts_in[c, k] = part[j, kk]

            @pl.when(jnp.logical_not(own))
            def _(copy=copy):
                copy.start()

    for kk in range(2):
        rows = slice(kk * BLK, (kk + 1) * BLK)
        out = diag_ref[rows, :]
        for b in range(8):
            own = jnp.logical_and(jnp.logical_and(xor(c, b, 3) == r, c == b), k == kk)

            @pl.when(jnp.logical_not(own))
            def _(b=b, kk=kk):
                remote(
                    part.at[0, 0], parts_in.at[b, kk], part_send.at[0, 0], part_recv.at[b, kk], device(r, c, 1 - k)
                ).wait_recv()

            out = out - parts_in[b, kk]
        corner_ref[rows, :] = out

    @pl.when(jnp.logical_not(stays))
    def _():
        first.wait_send()
        third.wait_send()

    swap.wait_send()
    pair.wait_send()
    share.wait_send()
    for d in (1, 2, 3):
        for h in range(2):
            gather[d, h].wait_send()
    for i in range(1, 8):
        send_of(i, c).wait_send()
    for j in range(8):
        for kk in range(2):
            own, copy = corner_of(j, kk)

            @pl.when(jnp.logical_not(own))
            def _(copy=copy):
                copy.wait_send()


def local(selected_inverse, pattern, ltil, diag_inverse):
    dma = pltpu.SemaphoreType.DMA
    vmem, anywhere = pl.BlockSpec(memory_space=pltpu.VMEM), pl.BlockSpec(memory_space=pl.ANY)
    return pl.pallas_call(
        kernel,
        out_shape=(
            jax.ShapeDtypeStruct((ROWS, BLK), jnp.bfloat16),
            jax.ShapeDtypeStruct((2 * BLK, BLK), F32),
        ),
        in_specs=[anywhere, pl.BlockSpec(memory_space=pltpu.SMEM), anywhere, vmem],
        out_specs=(vmem, vmem),
        scratch_shapes=[
            pltpu.VMEM((2, ROWS, HALF), jnp.bfloat16),
            pltpu.VMEM((8, ROWS, BLK), jnp.bfloat16),
            pltpu.VMEM((ROWS, 2 * BLK), F32),
            pltpu.VMEM((8, ROWS + PACKED, BLK), jnp.int16),
            pltpu.VMEM((8, ROWS + PACKED, BLK), jnp.int16),
            pltpu.VMEM((ROWS, BLK), jnp.bfloat16),
            pltpu.VMEM((2, ROWS, BLK), jnp.bfloat16),
            pltpu.VMEM((8, 2, BLK, BLK), F32),
            pltpu.VMEM((8, 2, BLK, BLK), F32),
            dma((1,)), dma((1,)), dma((1,)), dma((1,)), dma((1,)), dma((1,)), dma((1,)),
            dma((6,)), dma((6,)), dma((8,)), dma((8,)), dma((2,)), dma((2,)), dma((8, 2)), dma((8, 2)),
        ],
        compiler_params=pltpu.CompilerParams(
            collective_id=0, has_side_effects=True, vmem_limit_bytes=56 * 1024 * 1024
        ),
        cost_estimate=pl.CostEstimate(flops=15_000_000_000, bytes_accessed=20_000_000, transcendentals=0),
    )(selected_inverse, pattern, ltil, diag_inverse)


def solution(mesh):
    placed = (P("row", "col"), P("row", "col"), P("row", "col"), P("row", "col"))
    return jax.shard_map(
        local,
        mesh=mesh,
        in_specs=placed,
        out_specs=(P("row", "col"), P("row", "col")),
        check_vma=False,
    )
```

time: 488 us -> 224 us (0.46)
  the two profiles are of different devices: /device:TPU:102 before, /device:TPU:91 now
where the time goes in v1:
time: 224 us
  Pallas kernels  218 us (97%)
  local copies, waits for them, and re-layouts  4.91 us (2%)
    pallas_call x1, Pallas kernels, local(): pl.pallas_call(kernel, out_shape=(jax.ShapeDtypeStruct((ROWS, BLK), jnp.b...  218 us
    unnamed x3, local copies, waits for them, and re-layouts  4.91 us

profile of v1, /device:TPU:91, one launch (start us, length us, event | category | flops | bytes accessed | tf_op | source)
XLA Modules:
  0.0 223.8 jit_solution(911003399942411154)
XLA Ops:
  0.6 1.4 copy.6.pat_ref
  2.0 218.3 %shard_map.59 = (bf16[2560,128]{1,0:T(8,128)(2,1)}, f32[256,128]{1,0:T(8,128)}) custom-call(bf16[2560,1280]{1,0:T(8,128)(2,1)} %a_ref.1, s32[20,10]{1,0:T(8,128)} %copy.6.pat_ref, bf16[2560,128]{1,0:T(8,128)(2,1)} %lt_ref.1, f32[256,128]{1,0:T(8,128)} %diag_ref.1), custom_call_target="tpu_custom_call" | custom-call | flops 15000000512 | bytes 20000000 | tf_op jit(solution)/shard_map/pallas_call | solution.py:255
  220.3 2.0 copy.9
  222.3 1.6 copy.10

commit v2 on v0

v2 whole, which is shorter than its diff:
```python
import jax
import jax.numpy as jnp
from jax import lax
from jax.experimental import pallas as pl
from jax.experimental.pallas import tpu as pltpu
from jax.sharding import PartitionSpec as P

MESH = pl.DeviceIdType.MESH
BLK = 128
ROWS = 2560
HALF = 1280
TILE = 640
TILES = 4
CODE = 16
F32 = jnp.float32
BF16 = jnp.bfloat16


def device(r, c, k):
    return (r, c * 2 + k)


def xor(a, b, bits):
    out = 0
    for i in range(bits):
        w = 1 << i
        out = out + w * (((a // w) + (b // w)) % 2)
    return out


def swizzle(c):
    return (c // 4) * 4 + ((c // 2 + c // 4) % 2) * 2 + c % 2


def code_of(most):
    return jnp.clip(jnp.floor(jnp.log2(32000.0 / most)), -120.0, 120.0)


def as_int16(values):
    return values.astype(jnp.int32).astype(jnp.int16)


def as_float(values):
    return values.astype(jnp.int32).astype(F32)


def unit_of(code):
    return jnp.exp2(-as_float(code)[0:1, :])


def kernel(
    a_ref, pat_ref, lt_ref, diag_ref,
    panel_ref, corner_ref,
    pat, a_all, b_all, b_turned, z_out, z_in, y_out, y_in, late_in, slabs, part, parts_in,
    a_sem, core_send, core_recv, first_send, first_recv, pair_send, pair_recv,
    x_send, x_recv, z_send, z_recv, y_send, y_recv, late_send, late_recv,
    slab_send, slab_recv, share_send, share_recv, part_send, part_recv,
):
    r = lax.axis_index("row")
    col = lax.axis_index("col")
    c, k = col // 2, col % 2
    x, yh = r // 2, r % 2
    yl, z = c // 4, c % 4
    home = xor(r, swizzle(c), 3)
    slab = swizzle(xor(r, c, 3))
    x_of = {0: x, 1: (x + 3) % 4, 2: (x + 1) % 4, 3: (x + 2) % 4}
    x_ahead = device(x_of[2] * 2 + yh, c, k)
    x_back = device(x_of[1] * 2 + yh, c, k)
    partner = device(x * 2 + 1 - yh, c, k)
    other = device(r, c, 1 - k)

    barrier = pltpu.get_barrier_semaphore()
    senders = [device(c, swizzle(xor(r, c, 3)), k), other, partner, x_ahead, x_back]
    for i in range(1, 8):
        senders.append(device(r, ((yl + i // 4) % 2) * 4 + xor(z, i % 4, 2), k))
    for b in range(8):
        for kk in range(2):
            senders.append(device(xor(swizzle(c), b, 3), b, kk))
    for s in senders:
        pl.semaphore_signal(barrier, inc=1, device_id=s, device_id_type=MESH)

    own_a = pltpu.make_async_copy(a_ref, a_all.at[k], a_sem.at[0])
    own_a.start()
    own_pat = pltpu.make_async_copy(pat_ref, pat, a_sem.at[1])
    own_pat.start()
    pl.semaphore_wait(barrier, len(senders))

    def remote(src, dst, send, recv, to):
        return pltpu.make_async_remote_copy(
            src_ref=src, dst_ref=dst, send_sem=send, recv_sem=recv, device_id=to, device_id_type=MESH
        )

    stays = jnp.logical_and(r == 0, c == 0)
    halves = [pl.ds(q * HALF, HALF) for q in range(2)]
    first = [
        remote(lt_ref.at[rows], b_all.at[0, rows], first_send.at[q], first_recv.at[q], device(home, r, k))
        for q, rows in enumerate(halves)
    ]

    @pl.when(jnp.logical_not(stays))
    def _():
        for copy in first:
            copy.start()

    @pl.when(stays)
    def _():
        for q, rows in enumerate(halves):
            pltpu.make_async_copy(lt_ref.at[rows], b_all.at[0, rows], first_recv.at[q]).start()

    own_a.wait()
    own_pat.wait()

    def mask(i, carry):
        rows = pl.ds(pl.multiple_of(i * BLK, BLK), BLK)
        for j in range(HALF // BLK):
            keep = jnp.full((BLK, BLK), pat[i, j].astype(F32), F32).astype(BF16)
            cols = slice(j * BLK, (j + 1) * BLK)
            a_all[k, rows, cols] = a_all[k, rows, cols] * keep
        return carry

    lax.fori_loop(0, ROWS // BLK, mask, 0)
    swap = remote(a_all.at[k], a_all.at[k], core_send.at[0], core_recv.at[0], other)
    swap.start()

    def piece(s, q):
        return b_all.at[s, pl.ds(q * HALF, HALF)]

    def along(d, h, q):
        if (d, h) == (3, 1):
            source, to = 6, partner
        else:
            source = {1: h, 2: h, 3: 2 if q == 0 else 4}[d]
            to = x_ahead if d == 1 or (d == 3 and q == 0) else x_back
        i = (d - 1) * 4 + h * 2 + q
        return remote(piece(source, q), piece(2 * d + h, q), x_send.at[i], x_recv.at[i], to)

    def spread(h, q):
        along(1, h, q).start()
        along(2, h, q).start()

    pair = [remote(piece(0, q), piece(1, q), pair_send.at[q], pair_recv.at[q], partner) for q in range(2)]
    for q in range(2):
        first[q].wait_recv()
        spread(0, q)
        pair[q].start()

    remote(a_all.at[1 - k], a_all.at[1 - k], core_send.at[0], core_recv.at[0], other).wait_recv()

    def relation(d, h):
        hi, lo = x_of[d] // 2, x_of[d] % 2
        return hi, ((hi + lo + yl) % 2) * 2 + (yh + h) % 2

    def z_copy(i, t):
        return remote(
            z_out.at[i, t], z_in.at[i, t], z_send.at[i, t], z_recv.at[i, t],
            device(r, yl * 4 + xor(z, i % 4, 2), k),
        )

    direct = x < 2
    late_z = [jnp.where(x_of[1] >= 2, relation(1, 1)[1], relation(2, 1)[1]), relation(3, 1)[1]]

    def late(i, t):
        return remote(
            z_out.at[4 + late_z[i], t], late_in.at[i, t], late_send.at[i, t], late_recv.at[i, t],
            device(r, (1 - yl) * 4 + xor(z, late_z[i], 2), k),
        )

    def y_copy(t):
        return remote(y_out.at[t], y_in.at[t], y_send.at[t], y_recv.at[t], device(r, (1 - yl) * 4 + z, k))

    def each_tile(body):
        def run(t, carry):
            body(t)
            return carry

        lax.fori_loop(0, TILES, run, 0)

    def rows_of(t):
        return pl.ds(pl.multiple_of(t * TILE, TILE), TILE)

    def packed(values):
        power = code_of(jnp.max(jnp.abs(values), axis=0, keepdims=True))
        code = as_int16(jnp.broadcast_to(power, (CODE, values.shape[1])))
        return as_int16(values * jnp.exp2(power)), code

    def step(slots):
        right = [
            jnp.concatenate([b_all[2 * d + h, s, :] for d, h in slots], axis=1)
            for s in (slice(0, HALF), slice(HALF, ROWS))
        ]

        to = [relation(d, h) for d, h in slots]
        at = [across * 4 + by for across, by in to]

        def multiply(t):
            rows = rows_of(t)
            out = jnp.dot(a_all[0, rows, :], right[0], preferred_element_type=F32)
            out = out + jnp.dot(a_all[1, rows, :], right[1], preferred_element_type=F32)
            scaled, code = packed(out)
            for i, slot in enumerate(slots):
                cols = slice(i * BLK, (i + 1) * BLK)
                z_out[at[i], t, 0:TILE, :] = scaled[:, cols]
                z_out[at[i], t, TILE:, :] = code[:, cols]
                moves = to[i][1] != 0
                if slot in ((1, 1), (2, 1), (3, 1)):
                    straight = to[i][0] == 1
                    moves = jnp.logical_and(moves, jnp.logical_not(straight))

                    @pl.when(straight)
                    def _(slot=slot):
                        late(0 if slot != (3, 1) else 1, t).start()

                @pl.when(moves)
                def _(i=i):
                    z_copy(at[i], t).start()

        each_tile(multiply)

    def turn(slots):
        for d, h in slots:
            s = 2 * d + h
            b_turned[s * BLK:(s + 1) * BLK, :] = b_all[s].T

    step([(0, 0)])
    along(1, 0, 0).wait_recv()
    along(3, 0, 0).start()
    pair[0].wait_recv()
    spread(1, 0)
    along(2, 0, 1).wait_recv()
    along(3, 0, 1).start()
    pair[1].wait_recv()
    spread(1, 1)
    step([(0, 1)])
    along(1, 0, 1).wait_recv()
    along(2, 0, 0).wait_recv()
    step([(1, 0), (2, 0)])
    for q in range(2):
        along(3, 0, q).wait_recv()
        along(3, 1, q).start()
    step([(3, 0)])
    turn([(0, 0), (0, 1), (1, 0), (2, 0), (3, 0)])
    for d in (1, 2):
        for q in range(2):
            along(d, 1, q).wait_recv()
    step([(1, 1), (2, 1)])
    for q in range(2):
        along(3, 1, q).wait_recv()
    step([(3, 1)])
    turn([(1, 1), (2, 1), (3, 1)])

    def parts_of(across, t):
        return [z_out.at[across * 4, t]] + [z_in.at[across * 4 + i, t] for i in range(1, 4)]

    def sum_of(refs, used=None):
        out = 0.0
        for i, ref in enumerate(refs):
            unit = unit_of(ref[TILE:, :])
            if used is not None:
                unit = jnp.where(used[i], unit, 0.0)
            out = out + as_float(ref[0:TILE, :]) * unit
        return out

    used_across = [
        jnp.logical_and(late_z[0] != i, jnp.logical_not(jnp.logical_and(direct, late_z[1] == i))) for i in range(4)
    ]

    def pass_on(t):
        for i in range(1, 4):
            @pl.when(used_across[i])
            def _(i=i):
                z_copy(4 + i, t).wait_recv()

        y_out[t, 0:TILE, :], y_out[t, TILE:, :] = packed(sum_of(parts_of(1, t), used_across))
        y_copy(t).start()

    each_tile(pass_on)

    def third(t):
        rows = rows_of(t)
        return remote(panel_ref.at[rows], slabs.at[k, rows], slab_send.at[t], slab_recv.at[t], device(home, r, k))

    def finish(t):
        for i in range(1, 4):
            z_copy(i, t).wait_recv()

        late(0, t).wait_recv()

        @pl.when(direct)
        def _():
            late(1, t).wait_recv()

        y_copy(t).wait_recv()
        rows = rows_of(t)
        out = sum_of(parts_of(0, t) + [y_in.at[t], late_in.at[0, t], late_in.at[1, t]], [True] * 6 + [direct])
        panel_ref[rows, :] = (-out).astype(BF16)

        @pl.when(jnp.logical_not(stays))
        def _():
            third(t).start()

        @pl.when(stays)
        def _():
            pltpu.make_async_copy(panel_ref.at[rows], slabs.at[k, rows], slab_recv.at[t]).start()

    each_tile(finish)

    def share(t, owner):
        rows = rows_of(t)
        return remote(slabs.at[owner, rows], slabs.at[owner, rows], share_send.at[t], share_recv.at[t], other)

    def hand_over(t):
        third(t).wait_recv()
        share(t, k).start()

    each_tile(hand_over)

    def corner_of(j, kk):
        d, h = j // 2, j % 2
        to = swizzle(xor(x_of[d] * 2 + (yh + h) % 2, c, 3))
        own = jnp.logical_and(jnp.logical_and(to == r, slab == c), k == kk)
        i = j * 2 + kk
        copy = remote(
            part.at[i], parts_in.at[c * 2 + k], part_send.at[i], part_recv.at[c * 2 + k], device(to, slab, kk)
        )
        return i, own, copy

    for t in range(TILES):
        share(t, 1 - k).wait_recv()
    right = jnp.concatenate([slabs[0], slabs[1]], axis=1)
    for j in range(8):
        out = jnp.dot(b_turned[j * BLK:(j + 1) * BLK, :], right, preferred_element_type=F32)
        scaled, code = packed(out)
        for kk in range(2):
            i, own, copy = corner_of(j, kk)
            part[i, 0:BLK, :] = scaled[:, kk * BLK:(kk + 1) * BLK]
            part[i, BLK:, :] = code[:, kk * BLK:(kk + 1) * BLK]

            @pl.when(own)
            def _(i=i):
                parts_in[c * 2 + k] = part[i]

            @pl.when(jnp.logical_not(own))
            def _(copy=copy):
                copy.start()

    for kk in range(2):
        rows = slice(kk * BLK, (kk + 1) * BLK)
        out = diag_ref[rows, :]
        for b in range(8):
            i = b * 2 + kk
            own = jnp.logical_and(jnp.logical_and(xor(swizzle(c), b, 3) == r, c == b), k == kk)

            @pl.when(jnp.logical_not(own))
            def _(i=i):
                remote(part.at[0], parts_in.at[i], part_send.at[0], part_recv.at[i], other).wait_recv()

            out = out - as_float(parts_in[i, 0:BLK, :]) * unit_of(parts_in[i, BLK:, :])
        corner_ref[rows, :] = out

    @pl.when(jnp.logical_not(stays))
    def _():
        for copy in first:
            copy.wait_send()

    swap.wait_send()
    for q in range(2):
        pair[q].wait_send()
        for d in (1, 2, 3):
            for h in range(2):
                along(d, h, q).wait_send()

    def drain(t):
        for i in (1, 2, 3, 5, 6, 7):
            @pl.when(True if i < 4 else used_across[i - 4])
            def _(i=i):
                z_copy(i, t).wait_send()

        late(0, t).wait_send()

        @pl.when(direct)
        def _():
            late(1, t).wait_send()

        @pl.when(jnp.logical_not(stays))
        def _():
            third(t).wait_send()

        y_copy(t).wait_send()
        share(t, k).wait_send()

    each_tile(drain)
    for j in range(8):
        for kk in range(2):
            _, own, copy = corner_of(j, kk)

            @pl.when(jnp.logical_not(own))
            def _(copy=copy):
                copy.wait_send()


def local(selected_inverse, pattern, ltil, diag_inverse):
    dma = pltpu.SemaphoreType.DMA
    vmem, anywhere = pl.BlockSpec(memory_space=pltpu.VMEM), pl.BlockSpec(memory_space=pl.ANY)
    return pl.pallas_call(
        kernel,
        out_shape=(
            jax.ShapeDtypeStruct((ROWS, BLK), BF16),
            jax.ShapeDtypeStruct((2 * BLK, BLK), F32),
        ),
        in_specs=[anywhere, anywhere, anywhere, vmem],
        out_specs=(vmem, vmem),
        scratch_shapes=[
            pltpu.SMEM((ROWS // BLK, HALF // BLK), jnp.int32),
            pltpu.VMEM((2, ROWS, HALF), BF16),
            pltpu.VMEM((8, ROWS, BLK), BF16),
            pltpu.VMEM((8 * BLK, ROWS), BF16),
            pltpu.VMEM((8, TILES, TILE + CODE, BLK), jnp.int16),
            pltpu.VMEM((8, TILES, TILE + CODE, BLK), jnp.int16),
            pltpu.VMEM((TILES, TILE + CODE, BLK), jnp.int16),
            pltpu.VMEM((TILES, TILE + CODE, BLK), jnp.int16),
            pltpu.VMEM((2, TILES, TILE + CODE, BLK), jnp.int16),
            pltpu.VMEM((2, ROWS, BLK), BF16),
            pltpu.VMEM((16, BLK + CODE, BLK), jnp.int16),
            pltpu.VMEM((16, BLK + CODE, BLK), jnp.int16),
            dma((2,)), dma((1,)), dma((1,)), dma((2,)), dma((2,)), dma((2,)), dma((2,)),
            dma((12,)), dma((12,)), dma((8, TILES)), dma((8, TILES)), dma((TILES,)), dma((TILES,)),
            dma((2, TILES)), dma((2, TILES)), dma((TILES,)), dma((TILES,)), dma((TILES,)), dma((TILES,)),
            dma((16,)), dma((16,)),
        ],
        compiler_params=pltpu.CompilerParams(
            collective_id=0, has_side_effects=True, vmem_limit_bytes=56 * 1024 * 1024
        ),
        cost_estimate=pl.CostEstimate(flops=15_000_000_000, bytes_accessed=20_000_000, transcendentals=0),
    )(selected_inverse, pattern, ltil, diag_inverse)


def solution(mesh):
    placed = (P("row", "col"), P("row", "col"), P("row", "col"), P("row", "col"))
    return jax.shard_map(
        local,
        mesh=mesh,
        in_specs=placed,
        out_specs=(P("row", "col"), P("row", "col")),
        check_vma=False,
    )
```

time: 488 us -> 171 us (0.35)
  waiting for transfers between devices: 412 us -> 0 us
  Pallas kernels: 0 us -> 165 us
  matrix products: 30.5 us -> 0 us
  local copies, waits for them, and re-layouts: 22.5 us -> 4.91 us
  between operations: 13.8 us -> 0.64 us
  starting transfers between devices: 4.91 us -> 0 us
    reduce_scatter x2 -> x0, waiting for transfers between devices: 190 us -> none  [the longest x1 116 us: local(): lax.psum_scatter(partial_panel, 'col', scatter_dimension=1, tiled=True)]
    pallas_call x0 -> x1, Pallas kernels: none -> 165 us  [local(): pl.pallas_call(kernel, out_shape=(jax.ShapeDtypeStruct((ROWS, BLK), BF16)...]
    all_gather x2 -> x0, waiting for transfers between devices: 152 us -> none  [the longest x1 82.1 us: local(): tall = lax.all_gather(ltil, 'row', axis=0, tiled=True)]
    all_to_all x1 -> x0, waiting for transfers between devices: 68.5 us -> none  [local(): lax.all_to_all(tall, 'col', split_axis=0, concat_axis=1, tiled=True)]
    dot_general x2 -> x0, matrix products: 30.5 us -> none  [the longest x1 24 us: local(): partial_panel = jnp.dot(masked, matched, preferred_element_type=jnp.float32)]
    all_to_all x1 -> x0, local copies, waits for them, and re-layouts: 7.88 us -> none  [local(): lax.all_to_all(tall, 'col', split_axis=0, concat_axis=1, tiled=True)]
    unnamed x9 -> x3, local copies, waits for them, and re-layouts: 10.4 us -> 4.91 us
  transfers between devices with their start and end apart: 5 -> 0, of which waited for: 5 -> 0; matrix products, arithmetic and copies ran while one was open for 2% -> 0% of each run, Pallas kernels for 0% -> 0%
where the time goes in v2:
time: 171 us
  Pallas kernels  165 us (96%)
  local copies, waits for them, and re-layouts  4.91 us (3%)
    pallas_call x1, Pallas kernels, local(): pl.pallas_call(kernel, out_shape=(jax.ShapeDtypeStruct((ROWS, BLK), BF16)...  165 us
    unnamed x3, local copies, waits for them, and re-layouts  4.91 us

profile of v2, /device:TPU:102, one launch (start us, length us, event | category | flops | bytes accessed | tf_op | source)
XLA Modules:
  0.0 170.6 jit_solution(14828860208607689724)
XLA Ops:
  0.6 1.4 copy.6.pat_ref
  2.0 165.0 %shard_map.59 = (bf16[2560,128]{1,0:T(8,128)(2,1)}, f32[256,128]{1,0:T(8,128)}) custom-call(bf16[2560,1280]{1,0:T(8,128)(2,1)} %a_ref.1, s32[20,10]{1,0:T(8,128)} %copy.6.pat_ref, bf16[2560,128]{1,0:T(8,128)(2,1)} %lt_ref.1, f32[256,128]{1,0:T(8,128)} %diag_ref.1), custom_call_target="tpu_custom_call" | custom-call | flops 15000000512 | bytes 20000000 | tf_op jit(solution)/shard_map/pallas_call | solution.py:404
  167.0 2.0 %copy.9 = bf16[2560,128]{1,0:T(8,128)(2,1)} copy(bf16[2560,128]{1,0:T(8,128)(2,1)} %get-tuple-element.4) | data formatting | bytes 1310720
  169.0 1.6 copy.10

commit v3 on v2

--- a/solution.py
+++ b/solution.py
@@ -51,9 +51,9 @@
 def kernel(
     a_ref, pat_ref, lt_ref, diag_ref,
     panel_ref, corner_ref,
-    pat, a_all, b_all, b_turned, z_out, z_in, y_out, y_in, late_in, slabs, part, parts_in,
+    pat, a_all, b_all, b_turned, z_out, z_in, y_out, y_in, slabs, corner, part, parts_in,
     a_sem, core_send, core_recv, first_send, first_recv, pair_send, pair_recv,
-    x_send, x_recv, z_send, z_recv, y_send, y_recv, late_send, late_recv,
+    x_send, x_recv, z_send, z_recv, y_send, y_recv,
     slab_send, slab_recv, share_send, share_recv, part_send, part_recv,
 ):
     r = lax.axis_index("row")
@@ -156,15 +156,6 @@
             device(r, yl * 4 + xor(z, i % 4, 2), k),
         )
 
-    direct = x < 2
-    late_z = [jnp.where(x_of[1] >= 2, relation(1, 1)[1], relation(2, 1)[1]), relation(3, 1)[1]]
-
-    def late(i, t):
-        return remote(
-            z_out.at[4 + late_z[i], t], late_in.at[i, t], late_send.at[i, t], late_recv.at[i, t],
-            device(r, (1 - yl) * 4 + xor(z, late_z[i], 2), k),
-        )
-
     def y_copy(t):
         return remote(y_out.at[t], y_in.at[t], y_send.at[t], y_recv.at[t], device(r, (1 - yl) * 4 + z, k))
 
@@ -176,50 +167,44 @@
         lax.fori_loop(0, TILES, run, 0)
 
     def rows_of(t):
-        return pl.ds(pl.multiple_of(t * TILE, TILE), TILE)
+        return pl.ds(t * TILE if isinstance(t, int) else pl.multiple_of(t * TILE, TILE), TILE)
 
     def packed(values):
         power = code_of(jnp.max(jnp.abs(values), axis=0, keepdims=True))
         code = as_int16(jnp.broadcast_to(power, (CODE, values.shape[1])))
         return as_int16(values * jnp.exp2(power)), code
 
-    def step(slots):
-        right = [
-            jnp.concatenate([b_all[2 * d + h, s, :] for d, h in slots], axis=1)
-            for s in (slice(0, HALF), slice(HALF, ROWS))
-        ]
-
-        to = [relation(d, h) for d, h in slots]
-        at = [across * 4 + by for across, by in to]
-
+    def step(*groups):
         def multiply(t):
+            for slots in groups:
+                multiply_group(t, slots)
+
+        def multiply_group(t, slots):
             rows = rows_of(t)
+            right = [
+                jnp.concatenate([b_all[2 * d + h, s, :] for d, h in slots], axis=1)
+                for s in (slice(0, HALF), slice(HALF, ROWS))
+            ]
             out = jnp.dot(a_all[0, rows, :], right[0], preferred_element_type=F32)
             out = out + jnp.dot(a_all[1, rows, :], right[1], preferred_element_type=F32)
             scaled, code = packed(out)
             for i, slot in enumerate(slots):
+                across, by = relation(*slot)
+                at = across * 4 + by
                 cols = slice(i * BLK, (i + 1) * BLK)
-                z_out[at[i], t, 0:TILE, :] = scaled[:, cols]
-                z_out[at[i], t, TILE:, :] = code[:, cols]
-                moves = to[i][1] != 0
-                if slot in ((1, 1), (2, 1), (3, 1)):
-                    straight = to[i][0] == 1
-                    moves = jnp.logical_and(moves, jnp.logical_not(straight))
-
-                    @pl.when(straight)
-                    def _(slot=slot):
-                        late(0 if slot != (3, 1) else 1, t).start()
-
-                @pl.when(moves)
-                def _(i=i):
-                    z_copy(at[i], t).start()
+                z_out[at, t, 0:TILE, :] = scaled[:, cols]
+                z_out[at, t, TILE:, :] = code[:, cols]
+                @pl.when(by != 0)
+                def _(at=at):
+                    z_copy(at, t).start()
 
         each_tile(multiply)
 
     def turn(slots):
         for d, h in slots:
             s = 2 * d + h
-            b_turned[s * BLK:(s + 1) * BLK, :] = b_all[s].T
+            for t in range(TILES):
+                b_turned[t, s * BLK:(s + 1) * BLK, :] = b_all[s, t * TILE:(t + 1) * TILE, :].T
 
     step([(0, 0)])
     along(1, 0, 0).wait_recv()
@@ -242,38 +227,25 @@
     for d in (1, 2):
         for q in range(2):
             along(d, 1, q).wait_recv()
-    step([(1, 1), (2, 1)])
     for q in range(2):
         along(3, 1, q).wait_recv()
-    step([(3, 1)])
-    turn([(1, 1), (2, 1), (3, 1)])
+    step([(1, 1), (2, 1)], [(3, 1)])
 
     def parts_of(across, t):
         return [z_out.at[across * 4, t]] + [z_in.at[across * 4 + i, t] for i in range(1, 4)]
 
-    def sum_of(refs, used=None):
+    def sum_of(refs):
         out = 0.0
-        for i, ref in enumerate(refs):
-            unit = unit_of(ref[TILE:, :])
-            if used is not None:
-                unit = jnp.where(used[i], unit, 0.0)
-            out = out + as_float(ref[0:TILE, :]) * unit
+        for ref in refs:
+            out = out + as_float(ref[0:TILE, :]) * unit_of(ref[TILE:, :])
         return out
 
-    used_across = [
-        jnp.logical_and(late_z[0] != i, jnp.logical_not(jnp.logical_and(direct, late_z[1] == i))) for i in range(4)
-    ]
-
     def pass_on(t):
-        for i in range(1, 4):
-            @pl.when(used_across[i])
-            def _(i=i):
-                z_copy(4 + i, t).wait_recv()
-
-        y_out[t, 0:TILE, :], y_out[t, TILE:, :] = packed(sum_of(parts_of(1, t), used_across))
+        for i in range(5, 8):
+            z_copy(i, t).wait_recv()
+
+        y_out[t, 0:TILE, :], y_out[t, TILE:, :] = packed(sum_of(parts_of(1, t)))
         y_copy(t).start()
-
-    each_tile(pass_on)
 
     def third(t):
         rows = rows_of(t)
@@ -283,15 +255,9 @@
         for i in range(1, 4):
             z_copy(i, t).wait_recv()
 
-        late(0, t).wait_recv()
-
-        @pl.when(direct)
-        def _():
-            late(1, t).wait_recv()
-
         y_copy(t).wait_recv()
         rows = rows_of(t)
-        out = sum_of(parts_of(0, t) + [y_in.at[t], late_in.at[0, t], late_in.at[1, t]], [True] * 6 + [direct])
+        out = sum_of(parts_of(0, t) + [y_in.at[t]])
         panel_ref[rows, :] = (-out).astype(BF16)
 
         @pl.when(jnp.logical_not(stays))
@@ -302,17 +268,29 @@
         def _():
             pltpu.make_async_copy(panel_ref.at[rows], slabs.at[k, rows], slab_recv.at[t]).start()
 
-    each_tile(finish)
+    for t in range(TILES + 1):
+        if t < TILES:
+            pass_on(t)
+        if t > 0:
+            finish(t - 1)
+    turn([(1, 1), (2, 1), (3, 1)])
 
     def share(t, owner):
         rows = rows_of(t)
         return remote(slabs.at[owner, rows], slabs.at[owner, rows], share_send.at[t], share_recv.at[t], other)
 
-    def hand_over(t):
-        third(t).wait_recv()
-        share(t, k).start()
-
-    each_tile(hand_over)
+    for t in range(TILES + 1):
+        if t < TILES:
+            third(t).wait_recv()
+            share(t, k).start()
+        if t > 0:
+            share(t - 1, 1 - k).wait_recv()
+            rows = slice((t - 1) * TILE, t * TILE)
+            right = jnp.concatenate([slabs[0, rows, :], slabs[1, rows, :]], axis=1)
+            for j in range(4):
+                span = slice(j * 2 * BLK, (j + 1) * 2 * BLK)
+                out = jnp.dot(b_turned[t - 1, span, :], right, preferred_element_type=F32)
+                corner[span, :] = out if t == 1 else corner[span, :] + out
 
     def corner_of(j, kk):
         d, h = j // 2, j % 2
@@ -324,12 +302,8 @@
         )
         return i, own, copy
 
-    for t in range(TILES):
-        share(t, 1 - k).wait_recv()
-    right = jnp.concatenate([slabs[0], slabs[1]], axis=1)
     for j in range(8):
-        out = jnp.dot(b_turned[j * BLK:(j + 1) * BLK, :], right, preferred_element_type=F32)
-        scaled, code = packed(out)
+        scaled, code = packed(corner[j * BLK:(j + 1) * BLK, :])
         for kk in range(2):
             i, own, copy = corner_of(j, kk)
             part[i, 0:BLK, :] = scaled[:, kk * BLK:(kk + 1) * BLK]
@@ -371,15 +345,8 @@
 
     def drain(t):
         for i in (1, 2, 3, 5, 6, 7):
-            @pl.when(True if i < 4 else used_across[i - 4])
-            def _(i=i):
-                z_copy(i, t).wait_send()
-
-        late(0, t).wait_send()
-
-        @pl.when(direct)
-        def _():
-            late(1, t).wait_send()
+            z_copy(i, t).wait_send()
+
 
         @pl.when(jnp.logical_not(stays))
         def _():
@@ -413,18 +380,18 @@
             pltpu.SMEM((ROWS // BLK, HALF // BLK), jnp.int32),
             pltpu.VMEM((2, ROWS, HALF), BF16),
             pltpu.VMEM((8, ROWS, BLK), BF16),
-            pltpu.VMEM((8 * BLK, ROWS), BF16),
+            pltpu.VMEM((TILES, 8 * BLK, TILE), BF16),
             pltpu.VMEM((8, TILES, TILE + CODE, BLK), jnp.int16),
             pltpu.VMEM((8, TILES, TILE + CODE, BLK), jnp.int16),
             pltpu.VMEM((TILES, TILE + CODE, BLK), jnp.int16),
             pltpu.VMEM((TILES, TILE + CODE, BLK), jnp.int16),
-            pltpu.VMEM((2, TILES, TILE + CODE, BLK), jnp.int16),
             pltpu.VMEM((2, ROWS, BLK), BF16),
+            pltpu.VMEM((8 * BLK, 2 * BLK), F32),
             pltpu.VMEM((16, BLK + CODE, BLK), jnp.int16),
             pltpu.VMEM((16, BLK + CODE, BLK), jnp.int16),
             dma((2,)), dma((1,)), dma((1,)), dma((2,)), dma((2,)), dma((2,)), dma((2,)),
             dma((12,)), dma((12,)), dma((8, TILES)), dma((8, TILES)), dma((TILES,)), dma((TILES,)),
-            dma((2, TILES)), dma((2, TILES)), dma((TILES,)), dma((TILES,)), dma((TILES,)), dma((TILES,)),
+            dma((TILES,)), dma((TILES,)), dma((TILES,)), dma((TILES,)),
             dma((16,)), dma((16,)),
         ],
         compiler_params=pltpu.CompilerParams(

time: 171 us -> 155 us (0.906)
  the two profiles are of different devices: /device:TPU:102 before, /device:TPU:101 now
where the time goes in v3:
time: 155 us; the launch traced here: 154 us
  Pallas kernels  149 us (96%)
  local copies, waits for them, and re-layouts  4.91 us (3%)
    pallas_call x1, Pallas kernels, local(): pl.pallas_call(kernel, out_shape=(jax.ShapeDtypeStruct((ROWS, BLK), BF16)...  149 us
    unnamed x3, local copies, waits for them, and re-layouts  4.91 us

profile of v3, /device:TPU:101, one launch (start us, length us, event | category | flops | bytes accessed | tf_op | source)
XLA Modules:
  0.0 154.4 jit_solution(11195637898690068160)
XLA Ops:
  0.6 1.4 copy.6.pat_ref
  2.0 148.9 %shard_map.59 = (bf16[2560,128]{1,0:T(8,128)(2,1)}, f32[256,128]{1,0:T(8,128)}) custom-call(bf16[2560,1280]{1,0:T(8,128)(2,1)} %a_ref.1, s32[20,10]{1,0:T(8,128)} %copy.6.pat_ref, bf16[2560,128]{1,0:T(8,128)(2,1)} %lt_ref.1, f32[256,128]{1,0:T(8,128)} %diag_ref.1), custom_call_target="tpu_custom_call" | custom-call | flops 15000000512 | bytes 20000000 | tf_op jit(solution)/shard_map/pallas_call | solution.py:371
  150.9 2.0 %copy.9 = bf16[2560,128]{1,0:T(8,128)(2,1)} copy(bf16[2560,128]{1,0:T(8,128)(2,1)} %get-tuple-element.4) | data formatting | bytes 1310720
  152.9 1.6 %copy.10 = f32[256,128]{1,0:T(8,128)} copy(f32[256,128]{1,0:T(8,128)} %get-tuple-element.5) | data formatting | bytes 262144

commit v4 on v3

--- a/solution.py
+++ b/solution.py
@@ -9,9 +9,12 @@
 BLK = 128
 ROWS = 2560
 HALF = 1280
+CODE = 16
 TILE = 640
 TILES = 4
-CODE = 16
+LAST = ROWS - (TILES - 1) * TILE
+PACKED = ROWS + TILES * CODE
+LATE = [(1, 1), (2, 1)]
 F32 = jnp.float32
 BF16 = jnp.bfloat16
 
@@ -44,6 +47,22 @@
     return values.astype(jnp.int32).astype(F32)
 
 
+def size_of(t):
+    return LAST if isinstance(t, int) and t == TILES - 1 else TILE
+
+
+def span_of(t, step, size):
+    return pl.ds(t * step if isinstance(t, int) else pl.multiple_of(t * step, CODE), size)
+
+
+def rows_of(t):
+    return span_of(t, TILE, size_of(t))
+
+
+def with_code(t):
+    return span_of(t, TILE + CODE, size_of(t) + CODE)
+
+
 def unit_of(code):
     return jnp.exp2(-as_float(code)[0:1, :])
 
@@ -51,7 +70,7 @@
 def kernel(
     a_ref, pat_ref, lt_ref, diag_ref,
     panel_ref, corner_ref,
-    pat, a_all, b_all, b_turned, z_out, z_in, y_out, y_in, slabs, corner, part, parts_in,
+    pat, a_all, b_all, b_turned, total, z_out, z_in, y_out, y_in, slabs, corner, part, parts_in,
     a_sem, core_send, core_recv, first_send, first_recv, pair_send, pair_recv,
     x_send, x_recv, z_send, z_recv, y_send, y_recv,
     slab_send, slab_recv, share_send, share_recv, part_send, part_recv,
@@ -113,7 +132,7 @@
     def mask(i, carry):
         rows = pl.ds(pl.multiple_of(i * BLK, BLK), BLK)
         for j in range(HALF // BLK):
-            keep = jnp.full((BLK, BLK), pat[i, j].astype(F32), F32).astype(BF16)
+            keep = jnp.full((BLK, BLK), pat[j, i].astype(F32), F32).astype(BF16)
             cols = slice(j * BLK, (j + 1) * BLK)
             a_all[k, rows, cols] = a_all[k, rows, cols] * keep
         return carry
@@ -150,14 +169,26 @@
         hi, lo = x_of[d] // 2, x_of[d] % 2
         return hi, ((hi + lo + yl) % 2) * 2 + (yh + h) % 2
 
+    merged = yh == 0
+    late_z = [
+        jnp.where(x_of[1] // 2 == across, relation(1, 1)[1], relation(2, 1)[1]) for across in range(2)
+    ]
+
     def z_copy(i, t):
+        by = i % 4
+        if isinstance(i, int):
+            hop = by if by != 2 else jnp.where(merged, xor(late_z[i // 4], 2, 2), 2)
+        else:
+            hop = jnp.where(
+                jnp.logical_and(by == 2, merged), xor(jnp.where(i // 4 == 0, late_z[0], late_z[1]), 2, 2), by
+            )
         return remote(
-            z_out.at[i, t], z_in.at[i, t], z_send.at[i, t], z_recv.at[i, t],
-            device(r, yl * 4 + xor(z, i % 4, 2), k),
+            z_out.at[i, with_code(t)], z_in.at[i, with_code(t)], z_send.at[i, t], z_recv.at[i, t],
+            device(r, yl * 4 + xor(z, hop, 2), k),
         )
 
     def y_copy(t):
-        return remote(y_out.at[t], y_in.at[t], y_send.at[t], y_recv.at[t], device(r, (1 - yl) * 4 + z, k))
+        return remote(y_out.at[with_code(t)], y_in.at[with_code(t)], y_send.at[t], y_recv.at[t], device(r, (1 - yl) * 4 + z, k))
 
     def each_tile(body):
         def run(t, carry):
@@ -166,13 +197,18 @@
 
         lax.fori_loop(0, TILES, run, 0)
 
-    def rows_of(t):
-        return pl.ds(t * TILE if isinstance(t, int) else pl.multiple_of(t * TILE, TILE), TILE)
 
     def packed(values):
         power = code_of(jnp.max(jnp.abs(values), axis=0, keepdims=True))
         code = as_int16(jnp.broadcast_to(power, (CODE, values.shape[1])))
         return as_int16(values * jnp.exp2(power)), code
+
+    def put(ref, t, scaled, code):
+        ref[with_code(t), :] = jnp.concatenate([scaled, code], axis=0)
+
+    def unpacked(ref, t):
+        ref = ref.at[with_code(t)]
+        return as_float(ref[0:size_of(t), :]), unit_of(ref[size_of(t):, :])
 
     def step(*groups):
         def multiply(t):
@@ -187,13 +223,26 @@
             ]
             out = jnp.dot(a_all[0, rows, :], right[0], preferred_element_type=F32)
             out = out + jnp.dot(a_all[1, rows, :], right[1], preferred_element_type=F32)
+            if slots == LATE:
+                held = total.at[0:size_of(t)]
+                held[...] = out
+
+                @pl.when(merged)
+                def _():
+                    for i, slot in enumerate(slots):
+                        at = relation(*slot)[0] * 4 + 2
+                        cols = slice(i * BLK, (i + 1) * BLK)
+                        z_copy(at, t).wait_recv()
+                        values, unit = unpacked(z_in.at[at], t)
+                        held[:, cols] = held[:, cols] + values * unit
+
+                out = held[...]
             scaled, code = packed(out)
             for i, slot in enumerate(slots):
                 across, by = relation(*slot)
                 at = across * 4 + by
                 cols = slice(i * BLK, (i + 1) * BLK)
-                z_out[at, t, 0:TILE, :] = scaled[:, cols]
-                z_out[at, t, TILE:, :] = code[:, cols]
+                put(z_out.at[at], t, scaled[:, cols], code[:, cols])
                 @pl.when(by != 0)
                 def _(at=at):
                     z_copy(at, t).start()
@@ -204,7 +253,7 @@
         for d, h in slots:
             s = 2 * d + h
             for t in range(TILES):
-                b_turned[t, s * BLK:(s + 1) * BLK, :] = b_all[s, t * TILE:(t + 1) * TILE, :].T
+                b_turned[t, s * BLK:(s + 1) * BLK, 0:size_of(t)] = b_all[s, rows_of(t), :].T
 
     step([(0, 0)])
     along(1, 0, 0).wait_recv()
@@ -229,22 +278,33 @@
             along(d, 1, q).wait_recv()
     for q in range(2):
         along(3, 1, q).wait_recv()
-    step([(1, 1), (2, 1)], [(3, 1)])
-
-    def parts_of(across, t):
-        return [z_out.at[across * 4, t]] + [z_in.at[across * 4 + i, t] for i in range(1, 4)]
-
-    def sum_of(refs):
+    turn([(1, 1), (2, 1), (3, 1)])
+    step(LATE, [(3, 1)])
+
+    def parts_of(across):
+        return [z_out.at[across * 4]] + [z_in.at[across * 4 + i] for i in range(1, 4)]
+
+    def sum_of(refs, t):
         out = 0.0
-        for ref in refs:
-            out = out + as_float(ref[0:TILE, :]) * unit_of(ref[TILE:, :])
+        for i, ref in enumerate(refs):
+            values, unit = unpacked(ref, t)
+            if i == 2:
+                unit = jnp.where(merged, 0.0, unit)
+            out = out + values * unit
         return out
 
+    def z_wait(across, t):
+        for i in (1, 3):
+            z_copy(across * 4 + i, t).wait_recv()
+
+        @pl.when(jnp.logical_not(merged))
+        def _():
+            z_copy(across * 4 + 2, t).wait_recv()
+
     def pass_on(t):
-        for i in range(5, 8):
-            z_copy(i, t).wait_recv()
-
-        y_out[t, 0:TILE, :], y_out[t, TILE:, :] = packed(sum_of(parts_of(1, t)))
+        z_wait(1, t)
+
+        put(y_out, t, *packed(sum_of(parts_of(1), t)))
         y_copy(t).start()
 
     def third(t):
@@ -252,12 +312,11 @@
         return remote(panel_ref.at[rows], slabs.at[k, rows], slab_send.at[t], slab_recv.at[t], device(home, r, k))
 
     def finish(t):
-        for i in range(1, 4):
-            z_copy(i, t).wait_recv()
+        z_wait(0, t)
 
         y_copy(t).wait_recv()
         rows = rows_of(t)
-        out = sum_of(parts_of(0, t) + [y_in.at[t]])
+        out = sum_of(parts_of(0) + [y_in], t)
         panel_ref[rows, :] = (-out).astype(BF16)
 
         @pl.when(jnp.logical_not(stays))
@@ -273,7 +332,6 @@
             pass_on(t)
         if t > 0:
             finish(t - 1)
-    turn([(1, 1), (2, 1), (3, 1)])
 
     def share(t, owner):
         rows = rows_of(t)
@@ -285,11 +343,11 @@
             share(t, k).start()
         if t > 0:
             share(t - 1, 1 - k).wait_recv()
-            rows = slice((t - 1) * TILE, t * TILE)
+            rows = rows_of(t - 1)
             right = jnp.concatenate([slabs[0, rows, :], slabs[1, rows, :]], axis=1)
             for j in range(4):
                 span = slice(j * 2 * BLK, (j + 1) * 2 * BLK)
-                out = jnp.dot(b_turned[t - 1, span, :], right, preferred_element_type=F32)
+                out = jnp.dot(b_turned[t - 1, span, 0:size_of(t - 1)], right, preferred_element_type=F32)
                 corner[span, :] = out if t == 1 else corner[span, :] + out
 
     def corner_of(j, kk):
@@ -365,10 +423,15 @@
                 copy.wait_send()
 
 
+def hand_back(panel_ref, corner_ref, panel_out, corner_out):
+    panel_out[...] = panel_ref[...]
+    corner_out[...] = corner_ref[...]
+
+
 def local(selected_inverse, pattern, ltil, diag_inverse):
     dma = pltpu.SemaphoreType.DMA
     vmem, anywhere = pl.BlockSpec(memory_space=pltpu.VMEM), pl.BlockSpec(memory_space=pl.ANY)
-    return pl.pallas_call(
+    panel, corner = pl.pallas_call(
         kernel,
         out_shape=(
             jax.ShapeDtypeStruct((ROWS, BLK), BF16),
@@ -377,14 +440,15 @@
         in_specs=[anywhere, anywhere, anywhere, vmem],
         out_specs=(vmem, vmem),
         scratch_shapes=[
-            pltpu.SMEM((ROWS // BLK, HALF // BLK), jnp.int32),
+            pltpu.SMEM((HALF // BLK, ROWS // BLK), jnp.int32),
             pltpu.VMEM((2, ROWS, HALF), BF16),
             pltpu.VMEM((8, ROWS, BLK), BF16),
             pltpu.VMEM((TILES, 8 * BLK, TILE), BF16),
-            pltpu.VMEM((8, TILES, TILE + CODE, BLK), jnp.int16),
-            pltpu.VMEM((8, TILES, TILE + CODE, BLK), jnp.int16),
-            pltpu.VMEM((TILES, TILE + CODE, BLK), jnp.int16),
-            pltpu.VMEM((TILES, TILE + CODE, BLK), jnp.int16),
+            pltpu.VMEM((TILE, 2 * BLK), F32),
+            pltpu.VMEM((8, PACKED, BLK), jnp.int16),
+            pltpu.VMEM((8, PACKED, BLK), jnp.int16),
+            pltpu.VMEM((PACKED, BLK), jnp.int16),
+            pltpu.VMEM((PACKED, BLK), jnp.int16),
             pltpu.VMEM((2, ROWS, BLK), BF16),
             pltpu.VMEM((8 * BLK, 2 * BLK), F32),
             pltpu.VMEM((16, BLK + CODE, BLK), jnp.int16),
@@ -398,7 +462,16 @@
             collective_id=0, has_side_effects=True, vmem_limit_bytes=56 * 1024 * 1024
         ),
         cost_estimate=pl.CostEstimate(flops=15_000_000_000, bytes_accessed=20_000_000, transcendentals=0),
-    )(selected_inverse, pattern, ltil, diag_inverse)
+    )(selected_inverse, pattern.T, ltil, diag_inverse)
+    return pl.pallas_call(
+        hand_back,
+        out_shape=(
+            jax.ShapeDtypeStruct((ROWS, BLK), BF16),
+            jax.ShapeDtypeStruct((2 * BLK, BLK), F32),
+        ),
+        in_specs=[vmem, vmem],
+        out_specs=(vmem, vmem),
+    )(panel, corner)
 
 
 def solution(mesh):

time: 155 us -> 147 us (0.948)
  the two profiles are of different devices: /device:TPU:101 before, /device:TPU:102 now
where the time goes in v4:
time: 147 us; the launch traced here: 146 us
  Pallas kernels  146 us (99%)
    pallas_call x1, Pallas kernels, local(): pl.pallas_call(kernel, out_shape=(jax.ShapeDtypeStruct((ROWS, BLK), BF16)...  144 us

profile of v4, /device:TPU:102, one launch (start us, length us, event | category | flops | bytes accessed | tf_op | source)
XLA Modules:
  0.0 146.5 jit_solution(2844956630053196801)
XLA Ops:
  0.6 143.8 %shard_map.59 = (bf16[2560,128]{1,0:T(8,128)(2,1)}, f32[256,128]{1,0:T(8,128)}) custom-call(bf16[2560,1280]{1,0:T(8,128)(2,1)} %a_ref.1, s32[10,20]{1,0:T(8,128)} %bitcast.1, bf16[2560,128]{1,0:T(8,128)(2,1)} %lt_ref.1, f32[256,128]{1,0:T(8,128)} %diag_ref.1), custom_call_target="tpu_custom_call" | custom-call | flops 15000000512 | bytes 20000000 | tf_op jit(solution)/shard_map/pallas_call | solution.py:434
  144.5 2.0 %shard_map.60 = (bf16[2560,128]{1,0:T(8,128)(2,1)}, f32[256,128]{1,0:T(8,128)}) custom-call(bf16[2560,128]{1,0:T(8,128)(2,1)} %get-tuple-element.4.panel_ref, f32[256,128]{1,0:T(8,128)} %get-tuple-element.5.corner_ref), custom_call_target="tpu_custom_call" | custom-call | tf_op jit(solution)/shard_map/pallas_call | solution.py:466

commit v5 on v4

--- a/solution.py
+++ b/solution.py
@@ -73,7 +73,7 @@
     pat, a_all, b_all, b_turned, total, z_out, z_in, y_out, y_in, slabs, corner, part, parts_in,
     a_sem, core_send, core_recv, first_send, first_recv, pair_send, pair_recv,
     x_send, x_recv, z_send, z_recv, y_send, y_recv,
-    slab_send, slab_recv, share_send, share_recv, part_send, part_recv,
+    slab_send, slab_recv, turn_send, turn_recv, part_send, part_recv,
 ):
     r = lax.axis_index("row")
     col = lax.axis_index("col")
@@ -93,8 +93,7 @@
     for i in range(1, 8):
         senders.append(device(r, ((yl + i // 4) % 2) * 4 + xor(z, i % 4, 2), k))
     for b in range(8):
-        for kk in range(2):
-            senders.append(device(xor(swizzle(c), b, 3), b, kk))
+        senders.append(device(xor(swizzle(c), b, 3), b, k))
     for s in senders:
         pl.semaphore_signal(barrier, inc=1, device_id=s, device_id_type=MESH)
 
@@ -249,11 +248,16 @@
 
         each_tile(multiply)
 
+    def turned(s, owner):
+        part_of = b_turned.at[owner, :, pl.ds(s * BLK, BLK)]
+        return remote(part_of, part_of, turn_send.at[s], turn_recv.at[s], other)
+
     def turn(slots):
         for d, h in slots:
             s = 2 * d + h
             for t in range(TILES):
-                b_turned[t, s * BLK:(s + 1) * BLK, 0:size_of(t)] = b_all[s, rows_of(t), :].T
+                b_turned[k, t, s * BLK:(s + 1) * BLK, :] = b_all[s, rows_of(t), :].T
+            turned(s, k).start()
 
     step([(0, 0)])
     along(1, 0, 0).wait_recv()
@@ -309,7 +313,7 @@
 
     def third(t):
         rows = rows_of(t)
-        return remote(panel_ref.at[rows], slabs.at[k, rows], slab_send.at[t], slab_recv.at[t], device(home, r, k))
+        return remote(panel_ref.at[rows], slabs.at[rows], slab_send.at[t], slab_recv.at[t], device(home, r, k))
 
     def finish(t):
         z_wait(0, t)
@@ -325,7 +329,7 @@
 
         @pl.when(stays)
         def _():
-            pltpu.make_async_copy(panel_ref.at[rows], slabs.at[k, rows], slab_recv.at[t]).start()
+            pltpu.make_async_copy(panel_ref.at[rows], slabs.at[rows], slab_recv.at[t]).start()
 
     for t in range(TILES + 1):
         if t < TILES:
@@ -333,61 +337,46 @@
         if t > 0:
             finish(t - 1)
 
-    def share(t, owner):
-        rows = rows_of(t)
-        return remote(slabs.at[owner, rows], slabs.at[owner, rows], share_send.at[t], share_recv.at[t], other)
-
-    for t in range(TILES + 1):
-        if t < TILES:
-            third(t).wait_recv()
-            share(t, k).start()
-        if t > 0:
-            share(t - 1, 1 - k).wait_recv()
-            rows = rows_of(t - 1)
-            right = jnp.concatenate([slabs[0, rows, :], slabs[1, rows, :]], axis=1)
+    for s in range(8):
+        turned(s, 1 - k).wait_recv()
+    for t in range(TILES):
+        third(t).wait_recv()
+        right = slabs[rows_of(t), :]
+        for kk in range(2):
             for j in range(4):
                 span = slice(j * 2 * BLK, (j + 1) * 2 * BLK)
-                out = jnp.dot(b_turned[t - 1, span, 0:size_of(t - 1)], right, preferred_element_type=F32)
-                corner[span, :] = out if t == 1 else corner[span, :] + out
-
-    def corner_of(j, kk):
-        d, h = j // 2, j % 2
-        to = swizzle(xor(x_of[d] * 2 + (yh + h) % 2, c, 3))
-        own = jnp.logical_and(jnp.logical_and(to == r, slab == c), k == kk)
-        i = j * 2 + kk
-        copy = remote(
-            part.at[i], parts_in.at[c * 2 + k], part_send.at[i], part_recv.at[c * 2 + k], device(to, slab, kk)
-        )
-        return i, own, copy
+                out = jnp.dot(b_turned[kk, t, span, :], right, preferred_element_type=F32)
+                corner[kk, span, :] = out if t == 0 else corner[kk, span, :] + out
+
+    def corner_of(j):
+        to = swizzle(xor(x_of[j // 2] * 2 + (yh + j % 2) % 2, c, 3))
+        own = jnp.logical_and(to == r, slab == c)
+        return own, remote(part.at[j], parts_in.at[c], part_send.at[j], part_recv.at[c], device(to, slab, k))
 
     for j in range(8):
-        scaled, code = packed(corner[j * BLK:(j + 1) * BLK, :])
-        for kk in range(2):
-            i, own, copy = corner_of(j, kk)
-            part[i, 0:BLK, :] = scaled[:, kk * BLK:(kk + 1) * BLK]
-            part[i, BLK:, :] = code[:, kk * BLK:(kk + 1) * BLK]
-
-            @pl.when(own)
-            def _(i=i):
-                parts_in[c * 2 + k] = part[i]
-
-            @pl.when(jnp.logical_not(own))
-            def _(copy=copy):
-                copy.start()
-
-    for kk in range(2):
-        rows = slice(kk * BLK, (kk + 1) * BLK)
-        out = diag_ref[rows, :]
-        for b in range(8):
-            i = b * 2 + kk
-            own = jnp.logical_and(jnp.logical_and(xor(swizzle(c), b, 3) == r, c == b), k == kk)
-
-            @pl.when(jnp.logical_not(own))
-            def _(i=i):
-                remote(part.at[0], parts_in.at[i], part_send.at[0], part_recv.at[i], other).wait_recv()
-
-            out = out - as_float(parts_in[i, 0:BLK, :]) * unit_of(parts_in[i, BLK:, :])
-        corner_ref[rows, :] = out
+        span = slice(j * BLK, (j + 1) * BLK)
+        scaled, code = packed(jnp.concatenate([corner[0, span, :], corner[1, span, :]], axis=0))
+        part[j] = jnp.concatenate([scaled, code], axis=0)
+        own, copy = corner_of(j)
+
+        @pl.when(own)
+        def _(j=j):
+            parts_in[c] = part[j]
+
+        @pl.when(jnp.logical_not(own))
+        def _(copy=copy):
+            copy.start()
+
+    out = diag_ref[...]
+    for b in range(8):
+        own = jnp.logical_and(xor(swizzle(c), b, 3) == r, c == b)
+
+        @pl.when(jnp.logical_not(own))
+        def _(b=b):
+            remote(part.at[0], parts_in.at[b], part_send.at[0], part_recv.at[b], other).wait_recv()
+
+        out = out - as_float(parts_in[b, 0:2 * BLK, :]) * unit_of(parts_in[b, 2 * BLK:, :])
+    corner_ref[...] = out
 
     @pl.when(jnp.logical_not(stays))
     def _():
@@ -411,16 +400,15 @@
             third(t).wait_send()
 
         y_copy(t).wait_send()
-        share(t, k).wait_send()
 
     each_tile(drain)
     for j in range(8):
-        for kk in range(2):
-            _, own, copy = corner_of(j, kk)
-
-            @pl.when(jnp.logical_not(own))
-            def _(copy=copy):
-                copy.wait_send()
+        turned(j, k).wait_send()
+        own, copy = corner_of(j)
+
+        @pl.when(jnp.logical_not(own))
+        def _(copy=copy):
+            copy.wait_send()
 
 
 def hand_back(panel_ref, corner_ref, panel_out, corner_out):
@@ -443,20 +431,20 @@
             pltpu.SMEM((HALF // BLK, ROWS // BLK), jnp.int32),
             pltpu.VMEM((2, ROWS, HALF), BF16),
             pltpu.VMEM((8, ROWS, BLK), BF16),
-            pltpu.VMEM((TILES, 8 * BLK, TILE), BF16),
+            pltpu.VMEM((2, TILES, 8 * BLK, TILE), BF16),
             pltpu.VMEM((TILE, 2 * BLK), F32),
             pltpu.VMEM((8, PACKED, BLK), jnp.int16),
             pltpu.VMEM((8, PACKED, BLK), jnp.int16),
             pltpu.VMEM((PACKED, BLK), jnp.int16),
             pltpu.VMEM((PACKED, BLK), jnp.int16),
-            pltpu.VMEM((2, ROWS, BLK), BF16),
-            pltpu.VMEM((8 * BLK, 2 * BLK), F32),
-            pltpu.VMEM((16, BLK + CODE, BLK), jnp.int16),
-            pltpu.VMEM((16, BLK + CODE, BLK), jnp.int16),
+            pltpu.VMEM((ROWS, BLK), BF16),
+            pltpu.VMEM((2, 8 * BLK, BLK), F32),
+            pltpu.VMEM((8, 2 * BLK + CODE, BLK), jnp.int16),
+            pltpu.VMEM((8, 2 * BLK + CODE, BLK), jnp.int16),
             dma((2,)), dma((1,)), dma((1,)), dma((2,)), dma((2,)), dma((2,)), dma((2,)),
             dma((12,)), dma((12,)), dma((8, TILES)), dma((8, TILES)), dma((TILES,)), dma((TILES,)),
-            dma((TILES,)), dma((TILES,)), dma((TILES,)), dma((TILES,)),
-            dma((16,)), dma((16,)),
+            dma((TILES,)), dma((TILES,)), dma((8,)), dma((8,)),
+            dma((8,)), dma((8,)),
         ],
         compiler_params=pltpu.CompilerParams(
             collective_id=0, has_side_effects=True, vmem_limit_bytes=56 * 1024 * 1024

time: 147 us -> 143 us (0.973); the launches traced: 146 us -> 140 us
  Pallas kernels: 146 us -> 139 us
    pallas_call x1, Pallas kernels: 144 us -> 137 us  [local(): pl.pallas_call(kernel, out_shape=(jax.ShapeDtypeStruct((ROWS, BLK), BF16)...]
where the time goes in v5:
time: 143 us; the launch traced here: 140 us
  Pallas kernels  139 us (97%)
    pallas_call x1, Pallas kernels, local(): pl.pallas_call(kernel, out_shape=(jax.ShapeDtypeStruct((ROWS, BLK), BF16)...  137 us

profile of v5, /device:TPU:102, one launch (start us, length us, event | category | flops | bytes accessed | tf_op | source)
XLA Modules:
  0.0 139.8 jit_solution(11320381028584394671)
XLA Ops:
  0.6 137.2 %shard_map.59 = (bf16[2560,128]{1,0:T(8,128)(2,1)}, f32[256,128]{1,0:T(8,128)}) custom-call(bf16[2560,1280]{1,0:T(8,128)(2,1)} %a_ref.1, s32[10,20]{1,0:T(8,128)} %bitcast.1, bf16[2560,128]{1,0:T(8,128)(2,1)} %lt_ref.1, f32[256,128]{1,0:T(8,128)} %diag_ref.1), custom_call_target="tpu_custom_call" | custom-call | flops 15000000512 | bytes 20000000 | tf_op jit(solution)/shard_map/pallas_call | solution.py:422
  137.8 2.0 %shard_map.60 = (bf16[2560,128]{1,0:T(8,128)(2,1)}, f32[256,128]{1,0:T(8,128)}) custom-call(bf16[2560,128]{1,0:T(8,128)(2,1)} %get-tuple-element.4.panel_ref, f32[256,128]{1,0:T(8,128)} %get-tuple-element.5.corner_ref), custom_call_target="tpu_custom_call" | custom-call | tf_op jit(solution)/shard_map/pallas_call | solution.py:454

commit v6 on v5

--- a/solution.py
+++ b/solution.py
@@ -15,6 +15,8 @@
 LAST = ROWS - (TILES - 1) * TILE
 PACKED = ROWS + TILES * CODE
 LATE = [(1, 1), (2, 1)]
+EARLY = [(3, 0)]
+KEPT = 2
 F32 = jnp.float32
 BF16 = jnp.bfloat16
 
@@ -70,7 +72,7 @@
 def kernel(
     a_ref, pat_ref, lt_ref, diag_ref,
     panel_ref, corner_ref,
-    pat, a_all, b_all, b_turned, total, z_out, z_in, y_out, y_in, slabs, corner, part, parts_in,
+    pat, a_all, b_all, b_turned, total, z_out, z_in, y_out, y_in, mine, slabs, corner, part, parts_in,
     a_sem, core_send, core_recv, first_send, first_recv, pair_send, pair_recv,
     x_send, x_recv, z_send, z_recv, y_send, y_recv,
     slab_send, slab_recv, turn_send, turn_recv, part_send, part_recv,
@@ -242,9 +244,21 @@
                 at = across * 4 + by
                 cols = slice(i * BLK, (i + 1) * BLK)
                 put(z_out.at[at], t, scaled[:, cols], code[:, cols])
-                @pl.when(by != 0)
+                moves = by != 0
+                if slot in EARLY:
+                    moves = jnp.logical_and(moves, jnp.logical_or(merged, t < KEPT))
+
+                @pl.when(moves)
                 def _(at=at):
                     z_copy(at, t).start()
+
+            if (3, 1) in slots:
+                for slot in EARLY:
+                    across, by = relation(*slot)
+
+                    @pl.when(jnp.logical_and(jnp.logical_and(by != 0, jnp.logical_not(merged)), t < TILES - KEPT))
+                    def _(at=across * 4 + by):
+                        z_copy(at, t + KEPT).start()
 
         each_tile(multiply)
 
@@ -280,10 +294,11 @@
     for d in (1, 2):
         for q in range(2):
             along(d, 1, q).wait_recv()
+    turn([(1, 1), (2, 1)])
     for q in range(2):
         along(3, 1, q).wait_recv()
-    turn([(1, 1), (2, 1), (3, 1)])
     step(LATE, [(3, 1)])
+    turn([(3, 1)])
 
     def parts_of(across):
         return [z_out.at[across * 4]] + [z_in.at[across * 4 + i] for i in range(1, 4)]
@@ -313,7 +328,7 @@
 
     def third(t):
         rows = rows_of(t)
-        return remote(panel_ref.at[rows], slabs.at[rows], slab_send.at[t], slab_recv.at[t], device(home, r, k))
+        return remote(mine.at[rows], slabs.at[rows], slab_send.at[t], slab_recv.at[t], device(home, r, k))
 
     def finish(t):
         z_wait(0, t)
@@ -321,6 +336,7 @@
         y_copy(t).wait_recv()
         rows = rows_of(t)
         out = sum_of(parts_of(0) + [y_in], t)
+        mine[rows, :] = (-out).astype(BF16)
         panel_ref[rows, :] = (-out).astype(BF16)
 
         @pl.when(jnp.logical_not(stays))
@@ -329,7 +345,7 @@
 
         @pl.when(stays)
         def _():
-            pltpu.make_async_copy(panel_ref.at[rows], slabs.at[rows], slab_recv.at[t]).start()
+            pltpu.make_async_copy(mine.at[rows], slabs.at[rows], slab_recv.at[t]).start()
 
     for t in range(TILES + 1):
         if t < TILES:
@@ -437,6 +453,7 @@
             pltpu.VMEM((8, PACKED, BLK), jnp.int16),
             pltpu.VMEM((PACKED, BLK), jnp.int16),
             pltpu.VMEM((PACKED, BLK), jnp.int16),
+            pltpu.VMEM((ROWS, BLK), BF16),
             pltpu.VMEM((ROWS, BLK), BF16),
             pltpu.VMEM((2, 8 * BLK, BLK), F32),
             pltpu.VMEM((8, 2 * BLK + CODE, BLK), jnp.int16),

time: 143 us -> 139 us (0.972); the launches traced: 140 us -> 139 us
  no operation moved by 1% of the time
where the time goes in v6:
time: 139 us
  Pallas kernels  138 us (99%)
    pallas_call x1, Pallas kernels, local(): pl.pallas_call(kernel, out_shape=(jax.ShapeDtypeStruct((ROWS, BLK), BF16)...  136 us

profile of v6, /device:TPU:102, one launch (start us, length us, event | category | flops | bytes accessed | tf_op | source)
XLA Modules:
  0.0 139.0 jit_solution(2609623148421353932)
XLA Ops:
  0.6 136.4 %shard_map.59 = (bf16[2560,128]{1,0:T(8,128)(2,1)}, f32[256,128]{1,0:T(8,128)}) custom-call(bf16[2560,1280]{1,0:T(8,128)(2,1)} %a_ref.1, s32[10,20]{1,0:T(8,128)} %bitcast.1, bf16[2560,128]{1,0:T(8,128)(2,1)} %lt_ref.1, f32[256,128]{1,0:T(8,128)} %diag_ref.1), custom_call_target="tpu_custom_call" | custom-call | flops 15000000512 | bytes 20000000 | tf_op jit(solution)/shard_map/pallas_call | solution.py:438
  137.0 2.0 %shard_map.60 = (bf16[2560,128]{1,0:T(8,128)(2,1)}, f32[256,128]{1,0:T(8,128)}) custom-call(bf16[2560,128]{1,0:T(8,128)(2,1)} %get-tuple-element.4.panel_ref, f32[256,128]{1,0:T(8,128)} %get-tuple-element.5.corner_ref), custom_call_target="tpu_custom_call" | custom-call | tf_op jit(solution)/shard_map/pallas_call | solution.py:471

commit v7 on v6

--- a/solution.py
+++ b/solution.py
@@ -427,9 +427,20 @@
             copy.wait_send()
 
 
-def hand_back(panel_ref, corner_ref, panel_out, corner_out):
-    panel_out[...] = panel_ref[...]
-    corner_out[...] = corner_ref[...]
+def hand_back(panel_ref, corner_ref, panel_out, corner_out, panel_held, corner_held, sem):
+    ways = [(corner_ref, corner_held, corner_out)]
+    for t in range(TILES):
+        rows = pl.ds(t * TILE, TILE)
+        ways.append((panel_ref.at[rows], panel_held.at[rows], panel_out.at[rows]))
+    reads = [pltpu.make_async_copy(a, b, sem.at[0, i]) for i, (a, b, _) in enumerate(ways)]
+    writes = [pltpu.make_async_copy(b, c, sem.at[1, i]) for i, (_, b, c) in enumerate(ways)]
+    for copy in reads:
+        copy.start()
+    for read, write in zip(reads, writes):
+        read.wait()
+        write.start()
+    for copy in writes:
+        copy.wait()
 
 
 def local(selected_inverse, pattern, ltil, diag_inverse):
@@ -474,8 +485,13 @@
             jax.ShapeDtypeStruct((ROWS, BLK), BF16),
             jax.ShapeDtypeStruct((2 * BLK, BLK), F32),
         ),
-        in_specs=[vmem, vmem],
-        out_specs=(vmem, vmem),
+        in_specs=[anywhere, anywhere],
+        out_specs=(anywhere, anywhere),
+        scratch_shapes=[
+            pltpu.VMEM((ROWS, BLK), BF16),
+            pltpu.VMEM((2 * BLK, BLK), F32),
+            dma((2, TILES + 1)),
+        ],
     )(panel, corner)
 
 

time: 139 us -> 139 us (level)
  no operation moved by 1% of the time
where the time goes in v7:
time: 139 us
  Pallas kernels  138 us (99%)
    pallas_call x1, Pallas kernels, local(): pl.pallas_call(kernel, out_shape=(jax.ShapeDtypeStruct((ROWS, BLK), BF16)...  136 us

profile of v7, /device:TPU:102, one launch (start us, length us, event | category | flops | bytes accessed | tf_op | source)
XLA Modules:
  0.0 139.0 jit_solution(16836964131610237769)
XLA Ops:
  0.6 136.4 %shard_map.59 = (bf16[2560,128]{1,0:T(8,128)(2,1)}, f32[256,128]{1,0:T(8,128)}) custom-call(bf16[2560,1280]{1,0:T(8,128)(2,1)} %a_ref.1, s32[10,20]{1,0:T(8,128)} %bitcast.1, bf16[2560,128]{1,0:T(8,128)(2,1)} %lt_ref.1, f32[256,128]{1,0:T(8,128)} %diag_ref.1), custom_call_target="tpu_custom_call" | custom-call | flops 15000000512 | bytes 20000000 | tf_op jit(solution)/shard_map/pallas_call | solution.py:449
  137.0 2.0 %shard_map.60 = (bf16[2560,128]{1,0:T(8,128)(2,1)}, f32[256,128]{1,0:T(8,128)}) custom-call(bf16[2560,128]{1,0:T(8,128)(2,1)} %get-tuple-element.4.panel_ref, f32[256,128]{1,0:T(8,128)} %get-tuple-element.5.corner_ref), custom_call_target="tpu_custom_call" | custom-call | tf_op jit(solution)/shard_map/pallas_call | solution.py:482
